TPU v7x, 32 devices: a whole 2x2x4 slice. The times are simulated.
32 devices in a mesh: dp: 4 (over y, x), frame: 8 (over z, core).
Axes of the slice: x: 2, y: 2, z: 4, core: 2. Of those that a mesh axis runs over, the one named last changes fastest.
Arguments:
- video: bfloat16 [4, 32, 8, 64, 256], P('dp', 'frame'), may hold values from -6 to 6
- saved: bfloat16 [4, 32, 8, 64, 256], P('dp', 'frame'), may hold values from -6 to 6
- grad_out: bfloat16 [4, 32, 8, 64, 256], P('dp', 'frame'), may hold values from -6 to 6
- spatial_w: bfloat16 [2304, 256], replicated, may hold values from -0.125 to 0.125
- temporal_w: bfloat16 [768, 256], replicated, may hold values from -0.21875 to 0.21875
Outputs:
- grad_video: bfloat16 [4, 32, 8, 64, 256], P('dp', 'frame')
- grad_spatial: float32 [2304, 256], P('frame', 'dp')
- grad_temporal: float32 [768, 256], P('frame', 'dp')
All inputs are finite; a program needn't handle non-finite values.
Results may differ from a plain program's by a relative error of at most 0.0049.
Values may be sent and summed in bfloat16 or wider, within the bound.
A program may use at most 64 MiB of HBM per device.

v0:
```python
import math

import jax
import jax.numpy as jnp
from jax import lax
from jax.sharding import PartitionSpec as P


def shifted_2(shard, axis, by):
    length = lax.axis_size(axis)
    pairs = [(i, i + by) for i in range(length) if 0 <= i + by < length]
    return lax.ppermute(shard, axis, pairs)


def shifted(source, row_off, col_off):
    height = source.shape[1]
    width = source.shape[2]
    padded = jnp.pad(source, ((0, 0), (1, 1), (1, 1), (0, 0)))
    return padded[:, 1 + row_off : 1 + row_off + height, 1 + col_off : 1 + col_off + width, :]


def temporal_back(grad_ext, saved_ext, frames, temporal_w, channels):
    lag_count = temporal_w.shape[0] // channels
    grad_now = grad_ext[:frames].reshape(-1, channels)
    hidden = jnp.zeros((grad_now.shape[0], channels), jnp.float32)
    blocks = []
    for lag in range(lag_count):
        weight_block = temporal_w[lag * channels : (lag + 1) * channels]
        later = grad_ext[lag : lag + frames].reshape(-1, channels)
        hidden = hidden + lax.dot_general(
            later, weight_block, (((1,), (1,)), ((), ())), preferred_element_type=jnp.float32
        )
        earlier = saved_ext[lag_count - 1 - lag : lag_count - 1 - lag + frames].reshape(
            -1, channels
        )
        blocks.append(
            lax.dot_general(
                earlier, grad_now, (((0,), (0,)), ((), ())), preferred_element_type=jnp.float32
            )
        )
    return (hidden.astype(jnp.bfloat16), jnp.concatenate(blocks, axis=0))


def spatial_back(video_clip, grad_hidden, spatial_w, channels):
    grad_flat = grad_hidden.reshape(-1, channels)
    result = jnp.zeros(grad_flat.shape, jnp.float32)
    blocks = []
    for row_off in (-1, 0, 1):
        for col_off in (-1, 0, 1):
            tap_index = (row_off + 1) * 3 + (col_off + 1)
            weight_block = spatial_w[tap_index * channels : (tap_index + 1) * channels]
            moved = shifted(grad_hidden, -row_off, -col_off).reshape(-1, channels)
            result = result + lax.dot_general(
                moved, weight_block, (((1,), (1,)), ((), ())), preferred_element_type=jnp.float32
            )
            patch = shifted(video_clip, row_off, col_off).reshape(-1, channels)
            blocks.append(
                lax.dot_general(
                    patch, grad_flat, (((0,), (0,)), ((), ())), preferred_element_type=jnp.float32
                )
            )
    return (result.astype(jnp.bfloat16).reshape(grad_hidden.shape), jnp.concatenate(blocks, axis=0))


def local(video, saved, grad_out, spatial_w, temporal_w):
    channels = spatial_w.shape[1]
    lag_count = temporal_w.shape[0] // channels
    video_slab = video[0]
    saved_slab = saved[0]
    grad_slab = grad_out[0]
    local_frames, height, width = (grad_slab.shape[0], grad_slab.shape[1], grad_slab.shape[2])
    grad_next = shifted_2(grad_slab[: lag_count - 1], "frame", -1)
    saved_prev = shifted_2(saved_slab[local_frames - (lag_count - 1) :], "frame", 1)
    grad_ext = jnp.concatenate([grad_slab, grad_next], axis=0)
    saved_ext = jnp.concatenate([saved_prev, saved_slab], axis=0)
    hidden, wt_part = temporal_back(grad_ext, saved_ext, local_frames, temporal_w, channels)
    hidden = hidden.reshape(grad_slab.shape)
    grad_input, ws_part = spatial_back(video_slab, hidden, spatial_w, channels)
    ws_rows, wt_rows = (
        lax.psum_scatter(ws_part, "frame", scatter_dimension=0, tiled=True),
        lax.psum_scatter(wt_part, "frame", scatter_dimension=0, tiled=True),
    )
    ws_owned, wt_owned = (
        lax.psum_scatter(ws_rows, "dp", scatter_dimension=1, tiled=True),
        lax.psum_scatter(wt_rows, "dp", scatter_dimension=1, tiled=True),
    )
    positions = lax.axis_size("dp") * lax.axis_size("frame") * local_frames * height * width
    factor = 1.0 / math.sqrt(float(positions))
    return (grad_input[None], ws_owned * factor, wt_owned * factor)


def solution(mesh):
    return jax.shard_map(
        local,
        mesh=mesh,
        in_specs=(
            P("dp", "frame", None, None, None),
            P("dp", "frame", None, None, None),
            P("dp", "frame", None, None, None),
            P(),
            P(),
        ),
        out_specs=(P("dp", "frame", None, None, None), P("frame", "dp"), P("frame", "dp")),
        check_vma=False,
    )
```

profile of v0, /device:TPU:0, one launch (start us, length us, event | category | flops | bytes accessed | tf_op | source)
XLA Modules:
  0.0 158.0 jit_solution(7300841075170219064)
XLA Ops:
  7.2 2.0 %slice_bitcast_fusion.1 = bf16[2,8,64,256]{3,2,1,0:T(8,128)(2,1)} fusion(bf16[1,4,8,64,256]{4,3,2,1,0:T(8,128)(2,1)} %param.7), kind=kLoop, calls=%fused_computation.49 | loop fusion | bytes 1048576 | tf_op jit(solution)/shard_map/slice | solution.py:72
  9.3 1.4 collective-permute-start
  10.7 1.1 slice_bitcast_fusion
  11.8 3.1 %collective-permute-start.1 = (bf16[2,8,64,256]{3,2,1,0:T(8,128)(2,1)S(1)}, bf16[2,8,64,256]{3,2,1,0:T(8,128)(2,1)S(1)}, u32[]{:S(2)}, u32[]{:S(2)}) collective-permute-start(bf16[2,8,64,256]{3,2,1,0:T(8,128)(2,1)S(1)} %slice_bitcast_fusion), channel_id=1, source_target_pairs={{0,1},{1,2},{2,3},{3,4},{4,5},{5,6},{6,7},{8,9},{9,10},{10,11},{11... | collective-permute-start | bytes 1572872 | tf_op jit(solution)/shard_map/ppermute | solution.py:12
  14.9 0.5 fusion.17
  15.3 0.5 convolution_bitcast_fusion
  15.8 0.3 copy-done.12
  16.1 4.7 %pad_slice_fusion = (bf16[4,8,64,256]{3,2,1,0:T(8,128)(2,1)}, bf16[4,8,64,256]{3,2,1,0:T(8,128)(2,1)}, bf16[4,8,64,256]{3,2,1,0:T(8,128)(2,1)}, bf16[4,8,64,256]...) fusion(bf16[4,8,64,256]{3,2,1,0:T(8,128)(2,1)S(1)} %bitcast.108), kind=kLoop, calls=%fused_computation.12 | loop fusion | bytes 9437184 | tf_op jit(solution)/shard_map/slice | solution.py:19
  20.9 0.5 fusion.21
  21.4 0.5 fusion.22
  21.9 1.0 pad_maximum_fusion.2
  23.0 1.3 pad_maximum_fusion.1
  24.3 0.5 convolution_add_fusion.9
  24.8 0.5 fusion
  25.2 0.7 copy-done.9
  26.0 0.5 convolution_dynamic-update-slice_fusion.7
  26.5 0.5 convolution_dynamic-update-slice_fusion.6
  27.3 0.5 convolution_dynamic-update-slice_fusion.5
  27.8 0.5 convolution_dynamic-update-slice_fusion.4
  28.3 0.2 copy-done.13
  28.6 0.5 fusion.2
  29.2 0.5 convolution_dynamic-update-slice_fusion.3
  29.6 0.2 copy-done.4
  29.9 0.5 convolution_dynamic-update-slice_fusion.2
  30.5 0.5 convolution_dynamic-update-slice_fusion.1
  30.9 0.2 copy-done.2
  31.2 0.5 convolution_dynamic-update-slice_fusion
  31.7 1.4 copy-done.10
  33.4 4.8 %pad_slice_fusion.8 = (bf16[4,8,64,256]{3,2,1,0:T(8,128)(2,1)S(1)}, bf16[4,8,64,256]{3,2,1,0:T(8,128)(2,1)S(1)}, bf16[4,8,64,256]{3,2,1,0:T(8,128)(2,1)S(1)}, bf...) fusion(bf16[4,8,64,256]{3,2,1,0:T(8,128)(2,1)S(1)} %bitcast.81), kind=kLoop, calls=%fused_computation.20 | loop fusion | bytes 9437184 | tf_op jit(solution)/shard_map/slice | solution.py:19
  38.1 0.5 fusion.13
  38.6 0.5 convolution_add_fusion.7
  39.1 0.5 convolution_add_fusion.6
  39.6 0.5 convolution_add_fusion.5
  40.0 0.5 convolution_add_fusion.4
  40.5 0.5 convolution_add_fusion.3
  41.0 18.4 %reduce-scatter.11.cloned.1.call-done = f32[96,256]{1,0:T(8,128)} async-done(((f32[768,256]{1,0:T(8,128)}), f32[96,256]{1,0:T(8,128)}) %reduce-scatter.11.cloned.1.call-update) | async-done | bytes 98320 | tf_op jit(solution)/shard_map/reduce_scatter | solution.py:81
  59.4 1.6 %copy.15 = f32[96,256]{0,1:T(8,128)} copy(f32[96,256]{1,0:T(8,128)} %reduce-scatter.11.cloned.1.call-done) | data formatting | bytes 196608
  61.1 3.0 %convolution_add_fusion.2 = f32[2048,256]{1,0:T(8,128)} fusion(f32[2048,256]{1,0:T(8,128)S(1)} %convolution_add_fusion.3, bf16[2048,256]{1,0:T(8,128)(2,1)} %bitcast.100, bf16[2304,256]{1,0:T(8,128)(2,1)} %param.8), kind=kOutput, calls=%fused_computation.2 | convolution fusion | flops 268959744 | bytes 5373952 | tf_op jit(solution)/shard_map/dot_general | solution.py:53
  64.2 32.4 %reduce-scatter.9.cloned.1.call-done = f32[288,256]{1,0:T(8,128)} async-done(((f32[2304,256]{1,0:T(8,128)}), f32[288,256]{1,0:T(8,128)}) %reduce-scatter.9.cloned.1.call-update) | async-done | bytes 294928 | tf_op jit(solution)/shard_map/reduce_scatter | solution.py:80
  96.5 1.9 %copy.13 = f32[288,256]{0,1:T(8,128)} copy(f32[288,256]{1,0:T(8,128)} %reduce-scatter.9.cloned.1.call-done) | data formatting | bytes 589824
  98.5 2.5 %convolution_add_fusion.1 = f32[2048,256]{1,0:T(8,128)S(1)} fusion(f32[2048,256]{1,0:T(8,128)} %convolution_add_fusion.2, bf16[2048,256]{1,0:T(8,128)(2,1)} %bitcast.99, bf16[2304,256]{1,0:T(8,128)(2,1)} %param.8), kind=kOutput, calls=%fused_computation.1 | convolution fusion | flops 268959744 | bytes 5373952 | tf_op jit(solution)/shard_map/dot_general | solution.py:53
  100.9 2.3 %fusion.1 = bf16[2048,256]{1,0:T(8,128)(2,1)} fusion(f32[2048,256]{1,0:T(8,128)S(1)} %convolution_add_fusion.1, bf16[2048,256]{1,0:T(8,128)(2,1)S(1)} %bitcast.98, bf16[2304,256]{1,0:T(8,128)(2,1)} %param.8), kind=kOutput, calls=%fused_computation.11 | convolution fusion | flops 269484032 | bytes 4325376 | tf_op jit(solution)/shard_map/dot_general | solution.py:53
  103.3 19.3 %reduce-scatter.15.cloned.1.call-done = f32[64,96]{1,0:T(8,128)} async-done(((f32[256,96]{1,0:T(8,128)}), f32[64,96]{1,0:T(8,128)}) %reduce-scatter.15.cloned.1.call-update) | async-done | bytes 24592
  122.6 0.8 copy.16
  123.4 0.7 copy.11
  124.1 25.5 %reduce-scatter.13.cloned.1.call-done = f32[64,288]{1,0:T(8,128)} async-done(((f32[256,288]{1,0:T(8,128)}), f32[64,288]{1,0:T(8,128)}) %reduce-scatter.13.cloned.1.call-update) | async-done | bytes 73744
  149.7 1.0 copy.14
  150.7 0.8 copy.10
  (37 shorter events, 1.1 us)
Async XLA Ops:
  7.2 7.7 %copy-start = (bf16[1,4,8,64,256]{4,3,2,1,0:T(8,128)(2,1)S(1)}, bf16[1,4,8,64,256]{4,3,2,1,0:T(8,128)(2,1)}, u32[]{:S(2)}) copy-start(bf16[1,4,8,64,256]{4,3,2,1,0:T(8,128)(2,1)} %param.7) | copy-start | bytes 3145732
  7.2 7.7 %copy-start.14 = (bf16[768,256]{1,0:T(8,128)(2,1)S(1)}, bf16[768,256]{1,0:T(8,128)(2,1)}, u32[]{:S(2)}) copy-start(bf16[768,256]{1,0:T(8,128)(2,1)} %param.9) | copy-start | bytes 1179652
  7.2 52.2 %reduce-scatter.11.cloned.1.call-start = ((), (), s32[]{:S(2)}) async-start(), calls=%async_computation.5 | async-start | bytes 884736 | tf_op jit(solution)/shard_map/reduce_scatter | solution.py:81
  9.3 6.1 %copy-start.1 = (bf16[1,4,8,64,256]{4,3,2,1,0:T(8,128)(2,1)S(1)}, bf16[1,4,8,64,256]{4,3,2,1,0:T(8,128)(2,1)}, u32[]{:S(2)}) copy-start(bf16[1,4,8,64,256]{4,3,2,1,0:T(8,128)(2,1)} %param.6) | copy-start | bytes 3145732
  9.3 13.7 %collective-permute-start = (bf16[2,8,64,256]{3,2,1,0:T(8,128)(2,1)}, bf16[2,8,64,256]{3,2,1,0:T(8,128)(2,1)}, u32[]{:S(2)}, u32[]{:S(2)}) collective-permute-start(bf16[2,8,64,256]{3,2,1,0:T(8,128)(2,1)} %slice_bitcast_fusion.1), channel_id=1, source_target_pairs={{1,0},{2,1},{3,2},{4,3},{5,4},{6,5},{7,6},{9,8},{10,9},{11,10},{12... | collective-permute-start | bytes 1572872 | tf_op jit(solution)/shard_map/ppermute | solution.py:12
  11.8 9.0 %collective-permute-start.1 = (bf16[2,8,64,256]{3,2,1,0:T(8,128)(2,1)S(1)}, bf16[2,8,64,256]{3,2,1,0:T(8,128)(2,1)S(1)}, u32[]{:S(2)}, u32[]{:S(2)}) collective-permute-start(bf16[2,8,64,256]{3,2,1,0:T(8,128)(2,1)S(1)} %slice_bitcast_fusion), channel_id=1, source_target_pairs={{0,1},{1,2},{2,3},{3,4},{4,5},{5,6},{6,7},{8,9},{9,10},{10,11},{11... | collective-permute-start | bytes 1572872 | tf_op jit(solution)/shard_map/ppermute | solution.py:12
  14.9 1.2 copy-start.12
  22.9 73.6 %reduce-scatter.9.cloned.1.call-start = ((), (), s32[]{:S(2)}) async-start(), calls=%async_computation.4 | async-start | bytes 2654208 | tf_op jit(solution)/shard_map/reduce_scatter | solution.py:80
  24.8 1.2 copy-start.9
  25.2 1.3 copy-start.8
  26.0 1.3 copy-start.7
  26.5 1.3 copy-start.6
  27.3 1.3 copy-start.13
  27.8 1.3 copy-start.5
  28.6 1.3 copy-start.4
  29.2 1.3 copy-start.3
  29.9 1.3 copy-start.2
  31.7 1.4 copy-start.10
  33.1 89.4 %reduce-scatter.15.cloned.1.call-start = ((), (), s32[]{:S(2)}) async-start(), calls=%async_computation.7 | async-start | bytes 163840
  33.4 4.8 %copy-start.11 = (bf16[2304,256]{1,0:T(8,128)(2,1)S(1)}, bf16[2304,256]{1,0:T(8,128)(2,1)}, u32[]{:S(2)}) copy-start(bf16[2304,256]{1,0:T(8,128)(2,1)} %param.8) | copy-start | bytes 3538948
  61.1 88.6 %reduce-scatter.13.cloned.1.call-start = ((), (), s32[]{:S(2)}) async-start(), calls=%async_computation.6 | async-start | bytes 491520
Sparse Core Ops, SparseCore 0:
  23.0 36.3 reduce-scatter.10
  61.8 34.6 reduce-scatter.8
  99.5 23.0 reduce-scatter.14
  125.2 24.4 reduce-scatter.12
where the time goes:
time: 159 us; the launch traced here: 158 us
  waiting for transfers between devices  95.7 us (60%)
  local copies, waits for them, and re-layouts  23 us (14%)
  matrix products  17.9 us (11%)
  between operations  14.1 us (9%)
  starting transfers between devices  4.82 us (3%)
  other arithmetic  2.47 us (2%)
    unnamed x6, waiting for transfers between devices  44.9 us
    reduce_scatter x1, waiting for transfers between devices, local(): lax.psum_scatter(ws_part, 'frame', scatter_dimension=0, tiled=True)  32.4 us
    reduce_scatter x1, waiting for transfers between devices, local(): lax.psum_scatter(wt_part, 'frame', scatter_dimension=0, tiled=True)  18.4 us
    dot_general x9, matrix products, spatial_back(): lax.dot_general(moved, weight_block, (((1,), (1,)), ((), ())), preferred_...  10.6 us
    unnamed x36, local copies, waits for them, and re-layouts  10.5 us
    slice x2, local copies, waits for them, and re-layouts, shifted(): padded[:, 1 + row_off:1 + row_off + height, 1 + col_off:1 + col_off + wid...  9.42 us
    ppermute x2, starting transfers between devices, shifted_2(): return lax.ppermute(shard, axis, pairs)  4.48 us
    dot_general x9, matrix products, spatial_back(): lax.dot_general(patch, grad_flat, (((0,), (0,)), ((), ())), preferred_ele...  4.4 us
  transfers between devices with their start and end apart: 6, of which 4 were waited for; matrix products, arithmetic and copies ran while one was open for 23% of the time, Pallas kernels for 0%

commit v1 on v0

v1 whole, which is shorter than its diff:
```python
import functools
import math

import jax
import jax.numpy as jnp
from jax import lax
from jax.experimental import pallas as pl
from jax.experimental.pallas import tpu as pltpu
from jax.sharding import PartitionSpec as P

F32 = jnp.float32
BF16 = jnp.bfloat16
MESH = pl.DeviceIdType.MESH
LANES = 128
CORES = 2


def nt(lhs, rhs):
    return lax.dot_general(lhs, rhs, (((1,), (1,)), ((), ())), preferred_element_type=F32)


def nn(lhs, rhs):
    return lax.dot_general(lhs, rhs, (((1,), (0,)), ((), ())), preferred_element_type=F32)


def kernel(
    nd, nf, width, factor,
    g_hbm, s_hbm, v_hbm, sw_hbm, tw_hbm,
    gv_hbm, ows, owt,
    gext, sv, vv, sw, tw, st, vt, hid, part, gv, s1, r1, s2, r2, s3, r3, own3,
    in_sem, out_sem, halo_send, halo_recv, send1, recv1, send2, recv2, send3, recv3,
):
    nz = nf // CORES
    frames, pixels, ch = v_hbm.shape
    lags = tw_hbm.shape[0] // ch
    taps = sw_hbm.shape[0] // ch
    rim = lags - 1
    early = frames - rim
    sw_rows = sw_hbm.shape[0]
    rw, rt = sw_rows // nf, tw_hbm.shape[0] // nf
    rows = rw + rt
    col = ch // nd
    fold = max(1, LANES // col)
    lane_w = col * fold
    prow = rows // fold

    di, fi = lax.axis_index("dp"), lax.axis_index("frame")
    core, zi = lax.rem(fi, CORES), fi // CORES
    mate = zi * CORES + (CORES - 1 - core)

    loads = []
    for i, (src, dst) in enumerate(
        ((g_hbm, gext.at[pl.ds(0, frames)]), (tw_hbm, tw), (s_hbm, sv), (v_hbm, vv), (sw_hbm, sw))
    ):
        copy = pltpu.make_async_copy(src, dst, in_sem.at[i])
        copy.start()
        loads.append(copy)

    barrier = pltpu.get_barrier_semaphore()
    greeted = [{"frame": mate}, {"frame": lax.rem(fi + 1, nf)}, {"frame": lax.rem(fi + nf - 1, nf)}]
    greeted += [{"dp": lax.rem(di + k, nd)} for k in range(1, nd)]
    greeted += [{"frame": lax.rem(zi + k, nz) * CORES + core} for k in range(1, nz)]
    for device in greeted:
        pl.semaphore_signal(barrier, inc=1, device_id=device, device_id_type=MESH)
    pl.semaphore_wait(barrier, len(greeted))

    halos = [
        pltpu.make_async_remote_copy(
            src_ref=g_hbm.at[i], dst_ref=gext.at[frames + i],
            send_sem=halo_send.at[i], recv_sem=halo_recv.at[i],
            device_id={"frame": lax.rem(fi + nf - 1, nf)}, device_id_type=MESH,
        )
        for i in range(rim)
    ]

    @pl.when(fi > 0)
    def _():
        for halo in halos:
            halo.start()

    @pl.when(fi == nf - 1)
    def _():
        gext[frames:] = jnp.zeros((rim, pixels, ch), BF16)

    blank = jnp.zeros((3, frames, width, ch), BF16)
    hid[:, :, :width] = blank
    hid[:, :, width + pixels:] = blank

    column = lax.rem(lax.broadcasted_iota(jnp.int32, (pixels, ch), 0), width)

    def hidden(s):
        later = jnp.concatenate([gext[s + k] for k in range(lags)], axis=1)
        weight = jnp.concatenate([tw[k * ch:(k + 1) * ch] for k in range(lags)], axis=1)
        value = nt(later, weight)
        for b in (-1, 0, 1):
            moved = value
            if b == 1:
                moved = jnp.where(column >= 1, pltpu.roll(value, 1, 0), 0.0)
            if b == -1:
                moved = jnp.where(column < width - 1, pltpu.roll(value, pixels - 1, 0), 0.0)
            hid[b + 1, s, width:width + pixels] = moved.astype(BF16)

    def moved_rows(a):
        return pl.ds(width - a * width, pixels)

    def grad_video(s):
        moved = jnp.concatenate(
            [hid[b + 1, s, moved_rows(a)] for a in (-1, 0, 1) for b in (-1, 0, 1)], axis=1
        )
        weight = jnp.concatenate([sw[t * ch:(t + 1) * ch] for t in range(taps)], axis=1)
        gv[s] = nt(moved, weight).astype(BF16)
        copy = pltpu.make_async_copy(gv.at[s], gv_hbm.at[s], out_sem.at[s])
        copy.start()
        return copy

    loads[0].wait()
    loads[1].wait()
    for s in range(early):
        hidden(s)
    loads[2].wait()
    for s in range(frames):
        st[:, s * pixels:(s + 1) * pixels] = sv[s].T
    for k in range(lags):
        part[sw_rows + k * ch:sw_rows + (k + 1) * ch] = nn(
            st[:, :(frames - k) * pixels], gext[k:frames].reshape(-1, ch)
        )
    loads[3].wait()
    for s in range(frames):
        vt[:, s * pixels:(s + 1) * pixels] = vv[s].T
    for a in (-1, 0, 1):
        for b in (-1, 0, 1):
            t = (a + 1) * 3 + b + 1
            part[t * ch:(t + 1) * ch] = nn(
                vt[:, :early * pixels],
                hid[b + 1, :early, width - a * width:width - a * width + pixels].reshape(-1, ch),
            )
    loads[4].wait()
    stores = [grad_video(s) for s in range(early)]

    for i in range(rim):
        @pl.when(fi < nf - 1)
        def _():
            halos[i].wait_recv()
        hidden(early + i)
    for k in range(1, lags):
        part[sw_rows + k * ch:sw_rows + (k + 1) * ch] += nn(
            st[:, (frames - k) * pixels:], gext[frames:frames + k].reshape(-1, ch)
        )

    def group_z(j):
        return lax.rem(zi + 1 + j, nz)

    def group_rows(j, owner_core):
        owner = group_z(j) * CORES + owner_core
        first = part[pl.ds(pl.multiple_of(owner * rw, math.gcd(rw, 256)), rw)]
        second = part[pl.ds(pl.multiple_of(sw_rows + owner * rt, math.gcd(rt, 256)), rt)]
        return jnp.concatenate([first, second], axis=0)

    def to_mate(j):
        s1[j] = group_rows(j, CORES - 1 - core).astype(BF16)
        copy = pltpu.make_async_remote_copy(
            src_ref=s1.at[j], dst_ref=r1.at[j], send_sem=send1.at[j], recv_sem=recv1.at[j],
            device_id={"frame": mate}, device_id_type=MESH,
        )
        copy.start()
        return copy

    start = group_z(0) * CORES * rw
    first_tap = start // ch
    lead = max((z * CORES * rw) % ch for z in range(nz))
    copies1 = []
    for i in range(taps):
        t = lax.rem(first_tap + i, taps)
        b = lax.rem(t, 3)
        top = pl.multiple_of(2 * width - (t // 3) * width, 16)
        spot = pl.ds(pl.multiple_of(t * ch, ch), ch)
        part[spot] += nn(
            vt[:, early * pixels:], hid[b, early:, pl.ds(top, pixels)].reshape(-1, ch)
        )
        while len(copies1) < nz and (
            i == taps - 1 or lead + (len(copies1) + 1) * CORES * rw <= (i + 1) * ch
        ):
            copies1.append(to_mate(len(copies1)))

    lane = lax.broadcasted_iota(jnp.int32, (prow, lane_w), 1)
    copies2 = []
    for j in range(nz):
        copies1[j].wait_recv()
        total = group_rows(j, core) + r1[j].astype(F32)
        for d in range(nd):
            tile, off = (d * col) // lane_w, (d * col) % lane_w
            piece = None
            for q in range(fold):
                block = total[q * prow:(q + 1) * prow, tile * lane_w:(tile + 1) * lane_w]
                turn = (q * col - off) % lane_w
                if turn:
                    block = pltpu.roll(block, turn, 1)
                piece = block if piece is None else jnp.where(lane >= q * col, block, piece)
            s2[d, j] = piece.astype(BF16)
        for k in range(1, nd):
            to = lax.rem(di + k, nd)
            copy = pltpu.make_async_remote_copy(
                src_ref=s2.at[to, j], dst_ref=r2.at[k - 1, j],
                send_sem=send2.at[k - 1, j], recv_sem=recv2.at[k - 1, j],
                device_id={"dp": to}, device_id_type=MESH,
            )
            copy.start()
            copies2.append(copy)

    stores += [grad_video(s) for s in range(early, frames)]

    copies3 = []
    for j in range(nz):
        for k in range(nd - 1):
            copies2[j * (nd - 1) + k].wait_recv()
        total = s2[di, j].astype(F32)
        for k in range(nd - 1):
            total = total + r2[k, j].astype(F32)
        if j == nz - 1:
            own3[...] = total
        else:
            s3[j] = total.astype(BF16)
            copy = pltpu.make_async_remote_copy(
                src_ref=s3.at[j], dst_ref=r3.at[j], send_sem=send3.at[j], recv_sem=recv3.at[j],
                device_id={"frame": group_z(j) * CORES + core}, device_id_type=MESH,
            )
            copy.start()
            copies3.append(copy)

    total = own3[...]
    for j in range(nz - 1):
        copies3[j].wait_recv()
        total = total + r3[j].astype(F32)
    total = total * factor
    total = jnp.concatenate([total[:, q * col:(q + 1) * col] for q in range(fold)], axis=0)
    ows[...] = total[:rw]
    owt[...] = total[rw:]

    for copy in stores:
        copy.wait()
    for copy in copies1 + copies2 + copies3:
        copy.wait_send()

    @pl.when(fi > 0)
    def _():
        for halo in halos:
            halo.wait_send()


def local(nd, nf, video, saved, grad_out, spatial_w, temporal_w):
    _, frames, height, width, ch = video.shape
    pixels = height * width
    nz = nf // CORES
    lags, taps = temporal_w.shape[0] // ch, spatial_w.shape[0] // ch
    rw, rt = spatial_w.shape[0] // nf, temporal_w.shape[0] // nf
    rows, col = rw + rt, ch // nd
    fold = max(1, LANES // col)
    prow, lane_w = rows // fold, col * fold
    slab = (frames, pixels, ch)
    factor = 1.0 / math.sqrt(float(nd * nf * frames * pixels))
    flops = 2 * frames * pixels * ch * ch * 2 * (lags + taps)
    anywhere = pl.BlockSpec(memory_space=pl.ANY)
    onchip = pl.BlockSpec(memory_space=pltpu.VMEM)
    dma = pltpu.SemaphoreType.DMA
    gv, gs, gt = pl.pallas_call(
        functools.partial(kernel, nd, nf, width, factor),
        out_shape=(
            jax.ShapeDtypeStruct(slab, BF16),
            jax.ShapeDtypeStruct((rw, col), F32),
            jax.ShapeDtypeStruct((rt, col), F32),
        ),
        in_specs=[anywhere] * 5,
        out_specs=(anywhere, onchip, onchip),
        scratch_shapes=[
            pltpu.VMEM((frames + lags - 1, pixels, ch), BF16),
            pltpu.VMEM(slab, BF16),
            pltpu.VMEM(slab, BF16),
            pltpu.VMEM(spatial_w.shape, BF16),
            pltpu.VMEM(temporal_w.shape, BF16),
            pltpu.VMEM((ch, frames * pixels), BF16),
            pltpu.VMEM((ch, frames * pixels), BF16),
            pltpu.VMEM((3, frames, pixels + 2 * width, ch), BF16),
            pltpu.VMEM((spatial_w.shape[0] + temporal_w.shape[0], ch), F32),
            pltpu.VMEM(slab, BF16),
            pltpu.VMEM((nz, rows, ch), BF16),
            pltpu.VMEM((nz, rows, ch), BF16),
            pltpu.VMEM((nd, nz, prow, lane_w), BF16),
            pltpu.VMEM((nd - 1, nz, prow, lane_w), BF16),
            pltpu.VMEM((nz - 1, prow, lane_w), BF16),
            pltpu.VMEM((nz - 1, prow, lane_w), BF16),
            pltpu.VMEM((prow, lane_w), F32),
            dma((5,)),
            dma((frames,)),
            dma((lags - 1,)),
            dma((lags - 1,)),
            dma((nz,)),
            dma((nz,)),
            dma((nd - 1, nz)),
            dma((nd - 1, nz)),
            dma((nz - 1,)),
            dma((nz - 1,)),
        ],
        compiler_params=pltpu.CompilerParams(
            collective_id=0, has_side_effects=True, vmem_limit_bytes=48 * 1024 * 1024
        ),
        cost_estimate=pl.CostEstimate(
            flops=flops, bytes_accessed=8 * frames * pixels * ch, transcendentals=0
        ),
        name="conv_backward",
    )(
        grad_out.reshape(slab), saved.reshape(slab), video.reshape(slab), spatial_w, temporal_w
    )
    return (gv.reshape(video.shape), gs, gt)


def solution(mesh):
    nd, nf = mesh.shape["dp"], mesh.shape["frame"]
    return jax.shard_map(
        functools.partial(local, nd, nf),
        mesh=mesh,
        in_specs=(
            P("dp", "frame", None, None, None),
            P("dp", "frame", None, None, None),
            P("dp", "frame", None, None, None),
            P(),
            P(),
        ),
        out_specs=(P("dp", "frame", None, None, None), P("frame", "dp"), P("frame", "dp")),
        check_vma=False,
    )
```

time: 159 us -> 38.1 us (0.24)
  waiting for transfers between devices: 95.7 us -> 0 us
  Pallas kernels: 0 us -> 28.8 us
  matrix products: 17.9 us -> 0 us
  local copies, waits for them, and re-layouts: 23 us -> 8.36 us
  between operations: 14.1 us -> 0.65 us
  starting transfers between devices: 4.82 us -> 0 us
  other arithmetic: 2.47 us -> 0 us
    reduce_scatter x2 -> x0, waiting for transfers between devices: 50.8 us -> none  [the longest x1 32.4 us: local(): lax.psum_scatter(ws_part, 'frame', scatter_dimension=0, tiled=True)]
    unnamed x6 -> x0, waiting for transfers between devices: 44.9 us -> none
    pallas_call x0 -> x1, Pallas kernels: none -> 28.8 us  [local(): pl.pallas_call(functools.partial(kernel, nd, nf, width, factor), out_shap...]
    dot_general x24 -> x0, matrix products: 17.9 us -> none  [the longest x9 10.6 us: spatial_back(): lax.dot_general(moved, weight_block, (((1,), (1,)), ((), ())), preferred_...]
    slice x4 -> x0, local copies, waits for them, and re-layouts: 12.5 us -> none  [the longest x2 9.42 us: shifted(): padded[:, 1 + row_off:1 + row_off + height, 1 + col_off:1 + col_off + wid...]
    ppermute x2 -> x0, starting transfers between devices: 4.48 us -> none  [shifted_2(): return lax.ppermute(shard, axis, pairs)]
    concatenate x3 -> x0, other arithmetic: 2.46 us -> none  [the longest x1 1.29 us: local(): grad_ext = jnp.concatenate([grad_slab, grad_next], axis=0)]
    unnamed x36 -> x13, local copies, waits for them, and re-layouts: 10.5 us -> 8.36 us
  transfers between devices with their start and end apart: 6 -> 0, of which waited for: 4 -> 0; matrix products, arithmetic and copies ran while one was open for 23% -> 0% of each run, Pallas kernels for 0% -> 0%
where the time goes in v1:
time: 38.1 us; the launch traced here: 37.8 us
  Pallas kernels  28.8 us (76%)
  local copies, waits for them, and re-layouts  8.36 us (22%)
  between operations  0.65 us (2%)
    pallas_call x1, Pallas kernels, local(): pl.pallas_call(functools.partial(kernel, nd, nf, width, factor), out_shap...  28.8 us
    unnamed x13, local copies, waits for them, and re-layouts  8.36 us

profile of v1, /device:TPU:0, one launch (start us, length us, event | category | flops | bytes accessed | tf_op | source)
XLA Modules:
  0.0 37.8 jit_solution(531912014807796510)
XLA Ops:
  0.6 0.0 copy-start
  0.6 1.3 %copy-done = bf16[2304,256]{1,0:T(8,128)(2,1)S(1)} copy-done((bf16[2304,256]{1,0:T(8,128)(2,1)S(1)}, bf16[2304,256]{1,0:T(8,128)(2,1)}, u32[]{:S(2)}) %copy-start) | copy-done | bytes 1179672
  1.9 0.0 copy-start.1
  1.9 1.2 %copy-done.1 = bf16[1,4,8,64,256]{4,3,2,1,0:T(8,128)(2,1)S(1)} copy-done((bf16[1,4,8,64,256]{4,3,2,1,0:T(8,128)(2,1)S(1)}, bf16[1,4,8,64,256]{4,3,2,1,0:T(8,128)(2,1)}, u32[]{:S(2)}) %copy-start.1) | copy-done | bytes 1048600
  3.1 0.0 copy-start.2
  3.1 1.2 %copy-done.2 = bf16[1,4,8,64,256]{4,3,2,1,0:T(8,128)(2,1)S(1)} copy-done((bf16[1,4,8,64,256]{4,3,2,1,0:T(8,128)(2,1)S(1)}, bf16[1,4,8,64,256]{4,3,2,1,0:T(8,128)(2,1)}, u32[]{:S(2)}) %copy-start.2) | copy-done | bytes 1048600
  4.4 0.0 copy-start.3
  4.4 1.2 %copy-done.3 = bf16[1,4,8,64,256]{4,3,2,1,0:T(8,128)(2,1)S(1)} copy-done((bf16[1,4,8,64,256]{4,3,2,1,0:T(8,128)(2,1)S(1)}, bf16[1,4,8,64,256]{4,3,2,1,0:T(8,128)(2,1)}, u32[]{:S(2)}) %copy-start.3) | copy-done | bytes 1048600
  5.6 0.0 copy-start.4
  5.6 1.0 %copy-done.4 = bf16[768,256]{1,0:T(8,128)(2,1)S(1)} copy-done((bf16[768,256]{1,0:T(8,128)(2,1)S(1)}, bf16[768,256]{1,0:T(8,128)(2,1)}, u32[]{:S(2)}) %copy-start.4) | copy-done | bytes 393240
  6.6 28.8 %conv_backward.1 = (bf16[4,512,256]{2,1,0:T(8,128)(2,1)S(1)}, f32[288,64]{1,0:T(8,128)S(1)}, f32[96,64]{1,0:T(8,128)S(1)}) custom-call(bf16[4,512,256]{2,1,0:T(8,128)(2,1)S(1)} %bitcast.5, bf16[4,512,256]{2,1,0:T(8,128)(2,1)S(1)} %bitcast.6, bf16[4,512,256]{2,1,0:T(8,128)(2,1)S(1)} %bitcast.7, bf16[2304,256]{1,0:T(8,128)(2,1)S(1)} %copy-done, ...), custom_call_target="tpu_custom_call" | custom-call | flops 6442450944 | bytes 4194304 | tf_op jit(solution)/shard_map/conv_backward/pallas_call | solution.py:265
  35.4 0.7 %copy.9 = f32[96,64]{0,1:T(8,128)} copy(f32[96,64]{1,0:T(8,128)S(1)} %get-tuple-element.11) | data formatting | bytes 49152
  36.1 0.8 %copy.8 = f32[288,64]{0,1:T(8,128)} copy(f32[288,64]{1,0:T(8,128)S(1)} %get-tuple-element.10) | data formatting | bytes 147456
  36.8 1.0 %copy.11 = bf16[1,4,8,64,256]{4,3,2,1,0:T(8,128)(2,1)} copy(bf16[1,4,8,64,256]{4,3,2,1,0:T(8,128)(2,1)S(1)} %bitcast.4) | data formatting | bytes 2097152
Async XLA Ops:
  0.6 1.3 %copy-start = (bf16[2304,256]{1,0:T(8,128)(2,1)S(1)}, bf16[2304,256]{1,0:T(8,128)(2,1)}, u32[]{:S(2)}) copy-start(bf16[2304,256]{1,0:T(8,128)(2,1)} %sw_hbm.1) | copy-start | bytes 3538948
  1.9 1.2 %copy-start.1 = (bf16[1,4,8,64,256]{4,3,2,1,0:T(8,128)(2,1)S(1)}, bf16[1,4,8,64,256]{4,3,2,1,0:T(8,128)(2,1)}, u32[]{:S(2)}) copy-start(bf16[1,4,8,64,256]{4,3,2,1,0:T(8,128)(2,1)} %param.7) | copy-start | bytes 3145732
  3.1 1.2 %copy-start.2 = (bf16[1,4,8,64,256]{4,3,2,1,0:T(8,128)(2,1)S(1)}, bf16[1,4,8,64,256]{4,3,2,1,0:T(8,128)(2,1)}, u32[]{:S(2)}) copy-start(bf16[1,4,8,64,256]{4,3,2,1,0:T(8,128)(2,1)} %param.6) | copy-start | bytes 3145732
  4.4 1.2 %copy-start.3 = (bf16[1,4,8,64,256]{4,3,2,1,0:T(8,128)(2,1)S(1)}, bf16[1,4,8,64,256]{4,3,2,1,0:T(8,128)(2,1)}, u32[]{:S(2)}) copy-start(bf16[1,4,8,64,256]{4,3,2,1,0:T(8,128)(2,1)} %param.5) | copy-start | bytes 3145732
  5.6 1.0 %copy-start.4 = (bf16[768,256]{1,0:T(8,128)(2,1)S(1)}, bf16[768,256]{1,0:T(8,128)(2,1)}, u32[]{:S(2)}) copy-start(bf16[768,256]{1,0:T(8,128)(2,1)} %tw_hbm.1) | copy-start | bytes 1179652

commit v2 on v1

--- a/solution.py
+++ b/solution.py
@@ -13,10 +13,7 @@
 MESH = pl.DeviceIdType.MESH
 LANES = 128
 CORES = 2
-
-
-def nt(lhs, rhs):
-    return lax.dot_general(lhs, rhs, (((1,), (1,)), ((), ())), preferred_element_type=F32)
+VMEM_BYTES = 60 * 1024 * 1024
 
 
 def nn(lhs, rhs):
@@ -27,7 +24,7 @@
     nd, nf, width, factor,
     g_hbm, s_hbm, v_hbm, sw_hbm, tw_hbm,
     gv_hbm, ows, owt,
-    gext, sv, vv, sw, tw, st, vt, hid, part, gv, s1, r1, s2, r2, s3, r3, own3,
+    gext, sv, vv, sw, tw, swt, twt, st, vt, hid, part, gv, s1, r1, s2, r2, s3, r3, own3,
     in_sem, out_sem, halo_send, halo_recv, send1, recv1, send2, recv2, send3, recv3,
 ):
     nz = nf // CORES
@@ -90,8 +87,7 @@
 
     def hidden(s):
         later = jnp.concatenate([gext[s + k] for k in range(lags)], axis=1)
-        weight = jnp.concatenate([tw[k * ch:(k + 1) * ch] for k in range(lags)], axis=1)
-        value = nt(later, weight)
+        value = nn(later, twt[...])
         for b in (-1, 0, 1):
             moved = value
             if b == 1:
@@ -107,45 +103,57 @@
         moved = jnp.concatenate(
             [hid[b + 1, s, moved_rows(a)] for a in (-1, 0, 1) for b in (-1, 0, 1)], axis=1
         )
-        weight = jnp.concatenate([sw[t * ch:(t + 1) * ch] for t in range(taps)], axis=1)
-        gv[s] = nt(moved, weight).astype(BF16)
+        gv[s] = nn(moved, swt[...]).astype(BF16)
         copy = pltpu.make_async_copy(gv.at[s], gv_hbm.at[s], out_sem.at[s])
         copy.start()
         return copy
 
+    def temporal_grad(k, first, last):
+        return nn(
+            st[:, first * pixels:last * pixels], gext[first + k:last + k].reshape(-1, ch)
+        )
+
+    def spatial_grad(b, top, first, last):
+        return nn(
+            vt[:, first * pixels:last * pixels],
+            hid[b, first:last, pl.ds(top, pixels)].reshape(-1, ch),
+        )
+
+    def lag_rows(k):
+        return pl.ds(sw_rows + k * ch, ch)
+
+    loads[1].wait()
+    for k in range(lags):
+        twt[k * ch:(k + 1) * ch] = tw[k * ch:(k + 1) * ch].T
     loads[0].wait()
-    loads[1].wait()
     for s in range(early):
         hidden(s)
     loads[2].wait()
     for s in range(frames):
         st[:, s * pixels:(s + 1) * pixels] = sv[s].T
     for k in range(lags):
-        part[sw_rows + k * ch:sw_rows + (k + 1) * ch] = nn(
-            st[:, :(frames - k) * pixels], gext[k:frames].reshape(-1, ch)
-        )
+        part[lag_rows(k)] = temporal_grad(k, 0, frames - k)
     loads[3].wait()
     for s in range(frames):
         vt[:, s * pixels:(s + 1) * pixels] = vv[s].T
-    for a in (-1, 0, 1):
-        for b in (-1, 0, 1):
-            t = (a + 1) * 3 + b + 1
-            part[t * ch:(t + 1) * ch] = nn(
-                vt[:, :early * pixels],
-                hid[b + 1, :early, width - a * width:width - a * width + pixels].reshape(-1, ch),
-            )
+    for t in range(taps):
+        part[t * ch:(t + 1) * ch] = spatial_grad(t % 3, 2 * width - (t // 3) * width, 0, early)
     loads[4].wait()
-    stores = [grad_video(s) for s in range(early)]
+    for t in range(taps):
+        swt[t * ch:(t + 1) * ch] = sw[t * ch:(t + 1) * ch].T
 
     for i in range(rim):
         @pl.when(fi < nf - 1)
         def _():
             halos[i].wait_recv()
         hidden(early + i)
-    for k in range(1, lags):
-        part[sw_rows + k * ch:sw_rows + (k + 1) * ch] += nn(
-            st[:, (frames - k) * pixels:], gext[frames:frames + k].reshape(-1, ch)
-        )
+        for k in range(i + 1, lags):
+            part[lag_rows(k)] += temporal_grad(k, frames + i - k, frames + i - k + 1)
+        if i < rim - 1:
+            for t in range(taps):
+                part[t * ch:(t + 1) * ch] += spatial_grad(
+                    t % 3, 2 * width - (t // 3) * width, early + i, early + i + 1
+                )
 
     def group_z(j):
         return lax.rem(zi + 1 + j, nz)
@@ -165,26 +173,10 @@
         copy.start()
         return copy
 
-    start = group_z(0) * CORES * rw
-    first_tap = start // ch
-    lead = max((z * CORES * rw) % ch for z in range(nz))
-    copies1 = []
-    for i in range(taps):
-        t = lax.rem(first_tap + i, taps)
-        b = lax.rem(t, 3)
-        top = pl.multiple_of(2 * width - (t // 3) * width, 16)
-        spot = pl.ds(pl.multiple_of(t * ch, ch), ch)
-        part[spot] += nn(
-            vt[:, early * pixels:], hid[b, early:, pl.ds(top, pixels)].reshape(-1, ch)
-        )
-        while len(copies1) < nz and (
-            i == taps - 1 or lead + (len(copies1) + 1) * CORES * rw <= (i + 1) * ch
-        ):
-            copies1.append(to_mate(len(copies1)))
-
     lane = lax.broadcasted_iota(jnp.int32, (prow, lane_w), 1)
-    copies2 = []
-    for j in range(nz):
+    copies1, copies2, copies3, stores = [], [], [], []
+
+    def to_clips(j):
         copies1[j].wait_recv()
         total = group_rows(j, core) + r1[j].astype(F32)
         for d in range(nd):
@@ -207,10 +199,7 @@
             copy.start()
             copies2.append(copy)
 
-    stores += [grad_video(s) for s in range(early, frames)]
-
-    copies3 = []
-    for j in range(nz):
+    def to_owner(j):
         for k in range(nd - 1):
             copies2[j * (nd - 1) + k].wait_recv()
         total = s2[di, j].astype(F32)
@@ -227,14 +216,36 @@
             copy.start()
             copies3.append(copy)
 
+    first_tap = group_z(0) * CORES * rw // ch
+    lead = max((z * CORES * rw) % ch for z in range(nz))
+    for i in range(taps):
+        t = lax.rem(first_tap + i, taps)
+        top = pl.multiple_of(2 * width - (t // 3) * width, 16)
+        spot = pl.ds(pl.multiple_of(t * ch, ch), ch)
+        part[spot] += spatial_grad(lax.rem(t, 3), top, frames - 1, frames)
+        while len(copies1) < nz and (
+            i == taps - 1 or lead + (len(copies1) + 1) * CORES * rw <= (i + 1) * ch
+        ):
+            copies1.append(to_mate(len(copies1)))
+            if len(copies1) > 1:
+                to_clips(len(copies1) - 2)
+    stores.append(grad_video(0))
+    to_clips(nz - 1)
+    for j in range(nz):
+        if j + 1 < frames:
+            stores.append(grad_video(j + 1))
+        to_owner(j)
+    for s in range(nz + 1, frames):
+        stores.append(grad_video(s))
+
     total = own3[...]
     for j in range(nz - 1):
         copies3[j].wait_recv()
         total = total + r3[j].astype(F32)
     total = total * factor
     total = jnp.concatenate([total[:, q * col:(q + 1) * col] for q in range(fold)], axis=0)
-    ows[...] = total[:rw]
-    owt[...] = total[rw:]
+    ows[...] = total[:rw].T
+    owt[...] = total[rw:].T
 
     for copy in stores:
         copy.wait()
@@ -245,6 +256,17 @@
     def _():
         for halo in halos:
             halo.wait_send()
+
+
+def place(gv, gs, gt, gv_out, gs_out, gt_out, sem):
+    copies = [
+        pltpu.make_async_copy(src, dst, sem.at[i])
+        for i, (src, dst) in enumerate(((gv, gv_out), (gs, gs_out), (gt, gt_out)))
+    ]
+    for copy in copies:
+        copy.start()
+    for copy in copies:
+        copy.wait()
 
 
 def local(nd, nf, video, saved, grad_out, spatial_w, temporal_w):
@@ -266,8 +288,8 @@
         functools.partial(kernel, nd, nf, width, factor),
         out_shape=(
             jax.ShapeDtypeStruct(slab, BF16),
-            jax.ShapeDtypeStruct((rw, col), F32),
-            jax.ShapeDtypeStruct((rt, col), F32),
+            jax.ShapeDtypeStruct((col, rw), F32),
+            jax.ShapeDtypeStruct((col, rt), F32),
         ),
         in_specs=[anywhere] * 5,
         out_specs=(anywhere, onchip, onchip),
@@ -275,6 +297,8 @@
             pltpu.VMEM((frames + lags - 1, pixels, ch), BF16),
             pltpu.VMEM(slab, BF16),
             pltpu.VMEM(slab, BF16),
+            pltpu.VMEM(spatial_w.shape, BF16),
+            pltpu.VMEM(temporal_w.shape, BF16),
             pltpu.VMEM(spatial_w.shape, BF16),
             pltpu.VMEM(temporal_w.shape, BF16),
             pltpu.VMEM((ch, frames * pixels), BF16),
@@ -301,7 +325,7 @@
             dma((nz - 1,)),
         ],
         compiler_params=pltpu.CompilerParams(
-            collective_id=0, has_side_effects=True, vmem_limit_bytes=48 * 1024 * 1024
+            collective_id=0, has_side_effects=True, vmem_limit_bytes=VMEM_BYTES
         ),
         cost_estimate=pl.CostEstimate(
             flops=flops, bytes_accessed=8 * frames * pixels * ch, transcendentals=0
@@ -310,7 +334,16 @@
     )(
         grad_out.reshape(slab), saved.reshape(slab), video.reshape(slab), spatial_w, temporal_w
     )
-    return (gv.reshape(video.shape), gs, gt)
+    gv, gs, gt = pl.pallas_call(
+        place,
+        out_shape=tuple(jax.ShapeDtypeStruct(x.shape, x.dtype) for x in (gv, gs, gt)),
+        in_specs=[anywhere] * 3,
+        out_specs=(anywhere,) * 3,
+        scratch_shapes=[dma((3,))],
+        compiler_params=pltpu.CompilerParams(vmem_limit_bytes=VMEM_BYTES),
+        name="place_results",
+    )(gv, gs, gt)
+    return (gv.reshape(video.shape), gs.T, gt.T)
 
 
 def solution(mesh):

time: 38.1 us -> 65.9 us (1.73)
  Pallas kernels: 28.8 us -> 65.1 us
  local copies, waits for them, and re-layouts: 8.36 us -> 0 us
    pallas_call x0 -> x1, Pallas kernels: none -> 36.9 us  [local(): pl.pallas_call(place, out_shape=tuple((jax.ShapeDtypeStruct(x.shape, x.dt...]
    unnamed x13 -> x0, local copies, waits for them, and re-layouts: 8.36 us -> none
where the time goes in v2:
time: 65.9 us; the launch traced here: 65.7 us
  Pallas kernels  65.1 us (99%)
    pallas_call x1, Pallas kernels, local(): pl.pallas_call(place, out_shape=tuple((jax.ShapeDtypeStruct(x.shape, x.dt...  36.9 us
    pallas_call x1, Pallas kernels, local(): pl.pallas_call(functools.partial(kernel, nd, nf, width, factor), out_shap...  28.2 us

profile of v2, /device:TPU:0, one launch (start us, length us, event | category | flops | bytes accessed | tf_op | source)
XLA Modules:
  0.0 65.7 jit_solution(10430427911278014274)
XLA Ops:
  0.6 28.2 %conv_backward.1 = (bf16[4,512,256]{2,1,0:T(8,128)(2,1)}, f32[64,288]{1,0:T(8,128)}, f32[64,96]{1,0:T(8,128)}) custom-call(bf16[4,512,256]{2,1,0:T(8,128)(2,1)} %bitcast.6, bf16[4,512,256]{2,1,0:T(8,128)(2,1)} %bitcast.7, bf16[4,512,256]{2,1,0:T(8,128)(2,1)} %bitcast.8, bf16[2304,256]{1,0:T(8,128)(2,1)} %sw_hbm.1, bf16[768,256]{1,0:T(8,128)(2,1)} %tw_hbm.1), custom_call_target="tpu_custom_call" | custom-call | flops 6442450944 | bytes 4194304 | tf_op jit(solution)/shard_map/conv_backward/pallas_call | solution.py:287
  28.9 36.9 %place_results.1 = (bf16[4,512,256]{2,1,0:T(8,128)(2,1)}, f32[64,288]{1,0:T(8,128)}, f32[64,96]{1,0:T(8,128)}) custom-call(bf16[4,512,256]{2,1,0:T(8,128)(2,1)} %get-tuple-element.9.gv, f32[64,288]{1,0:T(8,128)} %get-tuple-element.10.gs, f32[64,96]{1,0:T(8,128)} %get-tuple-element.11.gt), custom_call_target="tpu_custom_call" | custom-call | tf_op jit(solution)/shard_map/place_results/pallas_call | solution.py:337

commit v3 on v2

--- a/solution.py
+++ b/solution.py
@@ -24,8 +24,8 @@
     nd, nf, width, factor,
     g_hbm, s_hbm, v_hbm, sw_hbm, tw_hbm,
     gv_hbm, ows, owt,
-    gext, sv, vv, sw, tw, swt, twt, st, vt, hid, part, gv, s1, r1, s2, r2, s3, r3, own3,
-    in_sem, out_sem, halo_send, halo_recv, send1, recv1, send2, recv2, send3, recv3,
+    gext, sv, vv, sw, tw, swt, twt, st, vt, hid, part, gv, s1, r1, s2, r2, s4, r4, half2, s3, r3, own3,
+    in_sem, out_sem, halo_send, halo_recv, send1, recv1, send2, recv2, send4, recv4, send3, recv3,
 ):
     nz = nf // CORES
     frames, pixels, ch = v_hbm.shape
@@ -138,10 +138,6 @@
         vt[:, s * pixels:(s + 1) * pixels] = vv[s].T
     for t in range(taps):
         part[t * ch:(t + 1) * ch] = spatial_grad(t % 3, 2 * width - (t // 3) * width, 0, early)
-    loads[4].wait()
-    for t in range(taps):
-        swt[t * ch:(t + 1) * ch] = sw[t * ch:(t + 1) * ch].T
-
     for i in range(rim):
         @pl.when(fi < nf - 1)
         def _():
@@ -174,10 +170,23 @@
         return copy
 
     lane = lax.broadcasted_iota(jnp.int32, (prow, lane_w), 1)
-    copies1, copies2, copies3, stores = [], [], [], []
+    copies1, copies2, copies3, copies4, stores = [], [], [], [], []
+
+    low = min(n for n in range(1, nd + 1) if nd % n == 0 and n * n >= nd)
+    high = nd // low
+    dx, dy = lax.rem(di, low), di // low
+
+    def split(j):
+        if j % 2 == 0:
+            return low, high, dx, dy
+        return high, low, dy, dx
+
+    def clip_device(j, a, b):
+        return {"dp": b * low + a if j % 2 == 0 else a * low + b}
 
     def to_clips(j):
         copies1[j].wait_recv()
+        na, nb, a, b = split(j)
         total = group_rows(j, core) + r1[j].astype(F32)
         for d in range(nd):
             tile, off = (d * col) // lane_w, (d * col) % lane_w
@@ -188,23 +197,50 @@
                 if turn:
                     block = pltpu.roll(block, turn, 1)
                 piece = block if piece is None else jnp.where(lane >= q * col, block, piece)
-            s2[d, j] = piece.astype(BF16)
-        for k in range(1, nd):
-            to = lax.rem(di + k, nd)
+            spot = (d % low) * high + d // low if j % 2 == 0 else d
+            s2[j, spot] = piece.astype(BF16)
+        sends = []
+        for k in range(1, na):
+            to = lax.rem(a + k, na)
             copy = pltpu.make_async_remote_copy(
-                src_ref=s2.at[to, j], dst_ref=r2.at[k - 1, j],
+                src_ref=s2.at[j, pl.ds(to * nb, nb)], dst_ref=r2.at[j, pl.ds((k - 1) * nb, nb)],
                 send_sem=send2.at[k - 1, j], recv_sem=recv2.at[k - 1, j],
-                device_id={"dp": to}, device_id_type=MESH,
+                device_id=clip_device(j, to, b), device_id_type=MESH,
             )
             copy.start()
-            copies2.append(copy)
+            sends.append(copy)
+        copies2.append(sends)
+
+    def to_half(j):
+        na, nb, a, b = split(j)
+        for copy in copies2[j]:
+            copy.wait_recv()
+
+        def summed(i):
+            total = s2[j, a * nb + i].astype(F32)
+            for k in range(na - 1):
+                total = total + r2[j, k * nb + i].astype(F32)
+            return total
+
+        half2[j] = summed(b)
+        sends = []
+        for k in range(1, nb):
+            to = lax.rem(b + k, nb)
+            s4[j, k - 1] = summed(to).astype(BF16)
+            copy = pltpu.make_async_remote_copy(
+                src_ref=s4.at[j, k - 1], dst_ref=r4.at[j, k - 1],
+                send_sem=send4.at[k - 1, j], recv_sem=recv4.at[k - 1, j],
+                device_id=clip_device(j, a, to), device_id_type=MESH,
+            )
+            copy.start()
+            sends.append(copy)
+        copies4.append(sends)
 
     def to_owner(j):
-        for k in range(nd - 1):
-            copies2[j * (nd - 1) + k].wait_recv()
-        total = s2[di, j].astype(F32)
-        for k in range(nd - 1):
-            total = total + r2[k, j].astype(F32)
+        total = half2[j]
+        for k, copy in enumerate(copies4[j]):
+            copy.wait_recv()
+            total = total + r4[j, k].astype(F32)
         if j == nz - 1:
             own3[...] = total
         else:
@@ -229,14 +265,21 @@
             copies1.append(to_mate(len(copies1)))
             if len(copies1) > 1:
                 to_clips(len(copies1) - 2)
+    to_clips(nz - 1)
+    loads[4].wait()
+    for t in range(taps):
+        swt[t * ch:(t + 1) * ch] = sw[t * ch:(t + 1) * ch].T
     stores.append(grad_video(0))
-    to_clips(nz - 1)
     for j in range(nz):
+        to_half(j)
         if j + 1 < frames:
             stores.append(grad_video(j + 1))
-        to_owner(j)
+        if j >= 2:
+            to_owner(j - 2)
     for s in range(nz + 1, frames):
         stores.append(grad_video(s))
+    for j in range(max(nz - 2, 0), nz):
+        to_owner(j)
 
     total = own3[...]
     for j in range(nz - 1):
@@ -249,7 +292,7 @@
 
     for copy in stores:
         copy.wait()
-    for copy in copies1 + copies2 + copies3:
+    for copy in sum(copies2 + copies4, copies1 + copies3):
         copy.wait_send()
 
     @pl.when(fi > 0)
@@ -258,14 +301,18 @@
             halo.wait_send()
 
 
-def place(gv, gs, gt, gv_out, gs_out, gt_out, sem):
-    copies = [
-        pltpu.make_async_copy(src, dst, sem.at[i])
-        for i, (src, dst) in enumerate(((gv, gv_out), (gs, gs_out), (gt, gt_out)))
-    ]
-    for copy in copies:
+def place(gv, gs, gt, gv_out, gs_out, gt_out, gv_held, gs_held, gt_held, in_sem, out_sem):
+    frames = gv.shape[0]
+    hops = [(gv.at[s], gv_held.at[s], gv_out.at[s]) for s in range(frames)]
+    hops += [(gs, gs_held, gs_out), (gt, gt_held, gt_out)]
+    inward = [pltpu.make_async_copy(a, b, in_sem.at[i]) for i, (a, b, _) in enumerate(hops)]
+    outward = [pltpu.make_async_copy(b, c, out_sem.at[i]) for i, (_, b, c) in enumerate(hops)]
+    for copy in inward:
         copy.start()
-    for copy in copies:
+    for first, second in zip(inward, outward):
+        first.wait()
+        second.start()
+    for copy in outward:
         copy.wait()
 
 
@@ -308,8 +355,11 @@
             pltpu.VMEM(slab, BF16),
             pltpu.VMEM((nz, rows, ch), BF16),
             pltpu.VMEM((nz, rows, ch), BF16),
-            pltpu.VMEM((nd, nz, prow, lane_w), BF16),
-            pltpu.VMEM((nd - 1, nz, prow, lane_w), BF16),
+            pltpu.VMEM((nz, nd, prow, lane_w), BF16),
+            pltpu.VMEM((nz, nd, prow, lane_w), BF16),
+            pltpu.VMEM((nz, nd, prow, lane_w), BF16),
+            pltpu.VMEM((nz, nd, prow, lane_w), BF16),
+            pltpu.VMEM((nz, prow, lane_w), F32),
             pltpu.VMEM((nz - 1, prow, lane_w), BF16),
             pltpu.VMEM((nz - 1, prow, lane_w), BF16),
             pltpu.VMEM((prow, lane_w), F32),
@@ -319,6 +369,8 @@
             dma((lags - 1,)),
             dma((nz,)),
             dma((nz,)),
+            dma((nd - 1, nz)),
+            dma((nd - 1, nz)),
             dma((nd - 1, nz)),
             dma((nd - 1, nz)),
             dma((nz - 1,)),
@@ -339,7 +391,8 @@
         out_shape=tuple(jax.ShapeDtypeStruct(x.shape, x.dtype) for x in (gv, gs, gt)),
         in_specs=[anywhere] * 3,
         out_specs=(anywhere,) * 3,
-        scratch_shapes=[dma((3,))],
+        scratch_shapes=[pltpu.VMEM(x.shape, x.dtype) for x in (gv, gs, gt)]
+        + [dma((frames + 2,)), dma((frames + 2,))],
         compiler_params=pltpu.CompilerParams(vmem_limit_bytes=VMEM_BYTES),
         name="place_results",
     )(gv, gs, gt)

time: 65.9 us -> 32.5 us (0.49)
  Pallas kernels: 65.1 us -> 31.7 us
    pallas_call x1, Pallas kernels: 36.9 us -> 2.05 us  [local(): pl.pallas_call(place, out_shape=tuple((jax.ShapeDtypeStruct(x.shape, x.dt...]
    pallas_call x1, Pallas kernels: 28.2 us -> 29.7 us  [local(): pl.pallas_call(functools.partial(kernel, nd, nf, width, factor), out_shap...]
where the time goes in v3:
time: 32.5 us; the launch traced here: 32.4 us
  Pallas kernels  31.7 us (98%)
  between operations  0.64 us (2%)
    pallas_call x1, Pallas kernels, local(): pl.pallas_call(functools.partial(kernel, nd, nf, width, factor), out_shap...  29.7 us
    pallas_call x1, Pallas kernels, local(): pl.pallas_call(place, out_shape=tuple((jax.ShapeDtypeStruct(x.shape, x.dt...  2.05 us

profile of v3, /device:TPU:0, one launch (start us, length us, event | category | flops | bytes accessed | tf_op | source)
XLA Modules:
  0.0 32.4 jit_solution(18123391473137099519)
XLA Ops:
  0.6 29.7 %conv_backward.1 = (bf16[4,512,256]{2,1,0:T(8,128)(2,1)}, f32[64,288]{1,0:T(8,128)}, f32[64,96]{1,0:T(8,128)}) custom-call(bf16[4,512,256]{2,1,0:T(8,128)(2,1)} %bitcast.6, bf16[4,512,256]{2,1,0:T(8,128)(2,1)} %bitcast.7, bf16[4,512,256]{2,1,0:T(8,128)(2,1)} %bitcast.8, bf16[2304,256]{1,0:T(8,128)(2,1)} %sw_hbm.1, bf16[768,256]{1,0:T(8,128)(2,1)} %tw_hbm.1), custom_call_target="tpu_custom_call" | custom-call | flops 6442450944 | bytes 4194304 | tf_op jit(solution)/shard_map/conv_backward/pallas_call | solution.py:334
  30.3 2.0 %place_results.1 = (bf16[4,512,256]{2,1,0:T(8,128)(2,1)}, f32[64,288]{1,0:T(8,128)}, f32[64,96]{1,0:T(8,128)}) custom-call(bf16[4,512,256]{2,1,0:T(8,128)(2,1)} %get-tuple-element.9.gv, f32[64,288]{1,0:T(8,128)} %get-tuple-element.10.gs, f32[64,96]{1,0:T(8,128)} %get-tuple-element.11.gt), custom_call_target="tpu_custom_call" | custom-call | tf_op jit(solution)/shard_map/place_results/pallas_call | solution.py:389

commit v4 on v2

--- a/solution.py
+++ b/solution.py
@@ -24,7 +24,7 @@
     nd, nf, width, factor,
     g_hbm, s_hbm, v_hbm, sw_hbm, tw_hbm,
     gv_hbm, ows, owt,
-    gext, sv, vv, sw, tw, swt, twt, st, vt, hid, part, gv, s1, r1, s2, r2, s3, r3, own3,
+    gext, sv, vv, sw, tw, swt, twt, st, vt, hid, part, gv, s1, r1, s2, r2, s3, r3, own3, gs, gt,
     in_sem, out_sem, halo_send, halo_recv, send1, recv1, send2, recv2, send3, recv3,
 ):
     nz = nf // CORES
@@ -104,9 +104,7 @@
             [hid[b + 1, s, moved_rows(a)] for a in (-1, 0, 1) for b in (-1, 0, 1)], axis=1
         )
         gv[s] = nn(moved, swt[...]).astype(BF16)
-        copy = pltpu.make_async_copy(gv.at[s], gv_hbm.at[s], out_sem.at[s])
-        copy.start()
-        return copy
+        pltpu.make_async_copy(gv.at[s], gv_hbm.at[s], out_sem.at[s]).start()
 
     def temporal_grad(k, first, last):
         return nn(
@@ -125,22 +123,43 @@
     loads[1].wait()
     for k in range(lags):
         twt[k * ch:(k + 1) * ch] = tw[k * ch:(k + 1) * ch].T
+    def loop(first, last):
+        return lambda body: lax.fori_loop(first, last, lambda i, _: (body(i), None)[1], None)
+
+    def tap_rows(t):
+        return pl.ds(pl.multiple_of(t * ch, ch), ch)
+
+    def tap_top(t):
+        return pl.multiple_of(2 * width - (t // 3) * width, 16)
+
+    def frame_lanes(s):
+        return pl.ds(pl.multiple_of(s * pixels, LANES), pixels)
+
     loads[0].wait()
-    for s in range(early):
-        hidden(s)
+    loop(0, early)(hidden)
     loads[2].wait()
-    for s in range(frames):
-        st[:, s * pixels:(s + 1) * pixels] = sv[s].T
+
+    @loop(0, frames)
+    def _(s):
+        st[:, frame_lanes(s)] = sv[s].T
+
     for k in range(lags):
         part[lag_rows(k)] = temporal_grad(k, 0, frames - k)
     loads[3].wait()
-    for s in range(frames):
-        vt[:, s * pixels:(s + 1) * pixels] = vv[s].T
-    for t in range(taps):
-        part[t * ch:(t + 1) * ch] = spatial_grad(t % 3, 2 * width - (t // 3) * width, 0, early)
+
+    @loop(0, frames)
+    def _(s):
+        vt[:, frame_lanes(s)] = vv[s].T
+
+    @loop(0, taps)
+    def _(t):
+        part[tap_rows(t)] = spatial_grad(lax.rem(t, 3), tap_top(t), 0, early)
+
     loads[4].wait()
-    for t in range(taps):
-        swt[t * ch:(t + 1) * ch] = sw[t * ch:(t + 1) * ch].T
+
+    @loop(0, taps)
+    def _(t):
+        swt[tap_rows(t)] = sw[tap_rows(t)].T
 
     for i in range(rim):
         @pl.when(fi < nf - 1)
@@ -150,9 +169,10 @@
         for k in range(i + 1, lags):
             part[lag_rows(k)] += temporal_grad(k, frames + i - k, frames + i - k + 1)
         if i < rim - 1:
-            for t in range(taps):
-                part[t * ch:(t + 1) * ch] += spatial_grad(
-                    t % 3, 2 * width - (t // 3) * width, early + i, early + i + 1
+            @loop(0, taps)
+            def _(t):
+                part[tap_rows(t)] += spatial_grad(
+                    lax.rem(t, 3), tap_top(t), early + i, early + i + 1
                 )
 
     def group_z(j):
@@ -218,25 +238,27 @@
 
     first_tap = group_z(0) * CORES * rw // ch
     lead = max((z * CORES * rw) % ch for z in range(nz))
-    for i in range(taps):
-        t = lax.rem(first_tap + i, taps)
-        top = pl.multiple_of(2 * width - (t // 3) * width, 16)
-        spot = pl.ds(pl.multiple_of(t * ch, ch), ch)
-        part[spot] += spatial_grad(lax.rem(t, 3), top, frames - 1, frames)
-        while len(copies1) < nz and (
-            i == taps - 1 or lead + (len(copies1) + 1) * CORES * rw <= (i + 1) * ch
-        ):
-            copies1.append(to_mate(len(copies1)))
-            if len(copies1) > 1:
-                to_clips(len(copies1) - 2)
-    stores.append(grad_video(0))
+    done = 0
+    for j in range(nz):
+        needed = -(-(lead + (j + 1) * CORES * rw) // ch)
+        needed = taps if j == nz - 1 else min(taps, needed)
+
+        @loop(done, needed)
+        def _(i):
+            t = lax.rem(first_tap + i, taps)
+            part[tap_rows(t)] += spatial_grad(lax.rem(t, 3), tap_top(t), frames - 1, frames)
+
+        done = needed
+        copies1.append(to_mate(j))
+        if j > 0:
+            to_clips(j - 1)
+    loop(0, early)(grad_video)
     to_clips(nz - 1)
+    loop(early, frames)(grad_video)
     for j in range(nz):
-        if j + 1 < frames:
-            stores.append(grad_video(j + 1))
         to_owner(j)
-    for s in range(nz + 1, frames):
-        stores.append(grad_video(s))
+    for s in range(frames):
+        stores.append(pltpu.make_async_copy(gv.at[s], gv_hbm.at[s], out_sem.at[s]))
 
     total = own3[...]
     for j in range(nz - 1):
@@ -244,8 +266,12 @@
         total = total + r3[j].astype(F32)
     total = total * factor
     total = jnp.concatenate([total[:, q * col:(q + 1) * col] for q in range(fold)], axis=0)
-    ows[...] = total[:rw].T
-    owt[...] = total[rw:].T
+    gs[...] = total[:rw].T
+    gt[...] = total[rw:].T
+    for i, (src, dst) in enumerate(((gs, ows), (gt, owt))):
+        copy = pltpu.make_async_copy(src, dst, out_sem.at[frames + i])
+        copy.start()
+        stores.append(copy)
 
     for copy in stores:
         copy.wait()
@@ -258,14 +284,18 @@
             halo.wait_send()
 
 
-def place(gv, gs, gt, gv_out, gs_out, gt_out, sem):
-    copies = [
-        pltpu.make_async_copy(src, dst, sem.at[i])
-        for i, (src, dst) in enumerate(((gv, gv_out), (gs, gs_out), (gt, gt_out)))
-    ]
-    for copy in copies:
+def place(gv, gs, gt, gv_out, gs_out, gt_out, gv_held, gs_held, gt_held, in_sem, out_sem):
+    frames = gv.shape[0]
+    hops = [(gv.at[s], gv_held.at[s], gv_out.at[s]) for s in range(frames)]
+    hops += [(gs, gs_held, gs_out), (gt, gt_held, gt_out)]
+    inward = [pltpu.make_async_copy(a, b, in_sem.at[i]) for i, (a, b, _) in enumerate(hops)]
+    outward = [pltpu.make_async_copy(b, c, out_sem.at[i]) for i, (_, b, c) in enumerate(hops)]
+    for copy in inward:
         copy.start()
-    for copy in copies:
+    for first, second in zip(inward, outward):
+        first.wait()
+        second.start()
+    for copy in outward:
         copy.wait()
 
 
@@ -282,7 +312,6 @@
     factor = 1.0 / math.sqrt(float(nd * nf * frames * pixels))
     flops = 2 * frames * pixels * ch * ch * 2 * (lags + taps)
     anywhere = pl.BlockSpec(memory_space=pl.ANY)
-    onchip = pl.BlockSpec(memory_space=pltpu.VMEM)
     dma = pltpu.SemaphoreType.DMA
     gv, gs, gt = pl.pallas_call(
         functools.partial(kernel, nd, nf, width, factor),
@@ -292,7 +321,7 @@
             jax.ShapeDtypeStruct((col, rt), F32),
         ),
         in_specs=[anywhere] * 5,
-        out_specs=(anywhere, onchip, onchip),
+        out_specs=(anywhere,) * 3,
         scratch_shapes=[
             pltpu.VMEM((frames + lags - 1, pixels, ch), BF16),
             pltpu.VMEM(slab, BF16),
@@ -313,8 +342,10 @@
             pltpu.VMEM((nz - 1, prow, lane_w), BF16),
             pltpu.VMEM((nz - 1, prow, lane_w), BF16),
             pltpu.VMEM((prow, lane_w), F32),
+            pltpu.VMEM((col, rw), F32),
+            pltpu.VMEM((col, rt), F32),
             dma((5,)),
-            dma((frames,)),
+            dma((frames + 2,)),
             dma((lags - 1,)),
             dma((lags - 1,)),
             dma((nz,)),
@@ -339,7 +370,8 @@
         out_shape=tuple(jax.ShapeDtypeStruct(x.shape, x.dtype) for x in (gv, gs, gt)),
         in_specs=[anywhere] * 3,
         out_specs=(anywhere,) * 3,
-        scratch_shapes=[dma((3,))],
+        scratch_shapes=[pltpu.VMEM(x.shape, x.dtype) for x in (gv, gs, gt)]
+        + [dma((frames + 2,)), dma((frames + 2,))],
         compiler_params=pltpu.CompilerParams(vmem_limit_bytes=VMEM_BYTES),
         name="place_results",
     )(gv, gs, gt)

time: 65.9 us -> 33.1 us (0.50)
  Pallas kernels: 65.1 us -> 32.3 us
    pallas_call x1, Pallas kernels: 36.9 us -> 2.05 us  [local(): pl.pallas_call(place, out_shape=tuple((jax.ShapeDtypeStruct(x.shape, x.dt...]
    pallas_call x1, Pallas kernels: 28.2 us -> 30.3 us  [local(): pl.pallas_call(functools.partial(kernel, nd, nf, width, factor), out_shap...]
where the time goes in v4:
time: 33.1 us; the launch traced here: 33 us
  Pallas kernels  32.3 us (98%)
  between operations  0.64 us (2%)
    pallas_call x1, Pallas kernels, local(): pl.pallas_call(functools.partial(kernel, nd, nf, width, factor), out_shap...  30.3 us
    pallas_call x1, Pallas kernels, local(): pl.pallas_call(place, out_shape=tuple((jax.ShapeDtypeStruct(x.shape, x.dt...  2.05 us

profile of v4, /device:TPU:0, one launch (start us, length us, event | category | flops | bytes accessed | tf_op | source)
XLA Modules:
  0.0 33.0 jit_solution(4348468585540354513)
XLA Ops:
  0.6 30.3 %conv_backward.1 = (bf16[4,512,256]{2,1,0:T(8,128)(2,1)}, f32[64,288]{1,0:T(8,128)}, f32[64,96]{1,0:T(8,128)}) custom-call(bf16[4,512,256]{2,1,0:T(8,128)(2,1)} %bitcast.6, bf16[4,512,256]{2,1,0:T(8,128)(2,1)} %bitcast.7, bf16[4,512,256]{2,1,0:T(8,128)(2,1)} %bitcast.8, bf16[2304,256]{1,0:T(8,128)(2,1)} %sw_hbm.1, bf16[768,256]{1,0:T(8,128)(2,1)} %tw_hbm.1), custom_call_target="tpu_custom_call" | custom-call | flops 6442450944 | bytes 4194304 | tf_op jit(solution)/shard_map/conv_backward/pallas_call | solution.py:316
  30.9 2.0 %place_results.1 = (bf16[4,512,256]{2,1,0:T(8,128)(2,1)}, f32[64,288]{1,0:T(8,128)}, f32[64,96]{1,0:T(8,128)}) custom-call(bf16[4,512,256]{2,1,0:T(8,128)(2,1)} %get-tuple-element.9.gv, f32[64,288]{1,0:T(8,128)} %get-tuple-element.10.gs, f32[64,96]{1,0:T(8,128)} %get-tuple-element.11.gt), custom_call_target="tpu_custom_call" | custom-call | tf_op jit(solution)/shard_map/place_results/pallas_call | solution.py:368

commit v5 on v3

--- a/solution.py
+++ b/solution.py
@@ -138,6 +138,9 @@
         vt[:, s * pixels:(s + 1) * pixels] = vv[s].T
     for t in range(taps):
         part[t * ch:(t + 1) * ch] = spatial_grad(t % 3, 2 * width - (t // 3) * width, 0, early)
+    loads[4].wait()
+    for t in range(taps):
+        swt[t * ch:(t + 1) * ch] = sw[t * ch:(t + 1) * ch].T
     for i in range(rim):
         @pl.when(fi < nf - 1)
         def _():
@@ -265,21 +268,17 @@
             copies1.append(to_mate(len(copies1)))
             if len(copies1) > 1:
                 to_clips(len(copies1) - 2)
+    stores.append(grad_video(0))
     to_clips(nz - 1)
-    loads[4].wait()
-    for t in range(taps):
-        swt[t * ch:(t + 1) * ch] = sw[t * ch:(t + 1) * ch].T
-    stores.append(grad_video(0))
     for j in range(nz):
         to_half(j)
+        if j > 0:
+            to_owner(j - 1)
         if j + 1 < frames:
             stores.append(grad_video(j + 1))
-        if j >= 2:
-            to_owner(j - 2)
     for s in range(nz + 1, frames):
         stores.append(grad_video(s))
-    for j in range(max(nz - 2, 0), nz):
-        to_owner(j)
+    to_owner(nz - 1)
 
     total = own3[...]
     for j in range(nz - 1):

time: 32.5 us -> 35.2 us (1.083)
  Pallas kernels: 31.7 us -> 34.4 us
    pallas_call x1, Pallas kernels: 29.7 us -> 32.3 us  [local(): pl.pallas_call(functools.partial(kernel, nd, nf, width, factor), out_shap...]
where the time goes in v5:
time: 35.2 us; the launch traced here: 35 us
  Pallas kernels  34.4 us (98%)
  between operations  0.64 us (2%)
    pallas_call x1, Pallas kernels, local(): pl.pallas_call(functools.partial(kernel, nd, nf, width, factor), out_shap...  32.3 us
    pallas_call x1, Pallas kernels, local(): pl.pallas_call(place, out_shape=tuple((jax.ShapeDtypeStruct(x.shape, x.dt...  2.05 us

profile of v5, /device:TPU:0, one launch (start us, length us, event | category | flops | bytes accessed | tf_op | source)
XLA Modules:
  0.0 35.0 jit_solution(13592686874065434109)
XLA Ops:
  0.6 32.3 %conv_backward.1 = (bf16[4,512,256]{2,1,0:T(8,128)(2,1)}, f32[64,288]{1,0:T(8,128)}, f32[64,96]{1,0:T(8,128)}) custom-call(bf16[4,512,256]{2,1,0:T(8,128)(2,1)} %bitcast.6, bf16[4,512,256]{2,1,0:T(8,128)(2,1)} %bitcast.7, bf16[4,512,256]{2,1,0:T(8,128)(2,1)} %bitcast.8, bf16[2304,256]{1,0:T(8,128)(2,1)} %sw_hbm.1, bf16[768,256]{1,0:T(8,128)(2,1)} %tw_hbm.1), custom_call_target="tpu_custom_call" | custom-call | flops 6442450944 | bytes 4194304 | tf_op jit(solution)/shard_map/conv_backward/pallas_call | solution.py:333
  32.9 2.0 %place_results.1 = (bf16[4,512,256]{2,1,0:T(8,128)(2,1)}, f32[64,288]{1,0:T(8,128)}, f32[64,96]{1,0:T(8,128)}) custom-call(bf16[4,512,256]{2,1,0:T(8,128)(2,1)} %get-tuple-element.9.gv, f32[64,288]{1,0:T(8,128)} %get-tuple-element.10.gs, f32[64,96]{1,0:T(8,128)} %get-tuple-element.11.gt), custom_call_target="tpu_custom_call" | custom-call | tf_op jit(solution)/shard_map/place_results/pallas_call | solution.py:388

commit v6 on v2

--- a/solution.py
+++ b/solution.py
@@ -16,6 +16,10 @@
 VMEM_BYTES = 60 * 1024 * 1024
 
 
+def nt(lhs, rhs):
+    return lax.dot_general(lhs, rhs, (((1,), (1,)), ((), ())), preferred_element_type=F32)
+
+
 def nn(lhs, rhs):
     return lax.dot_general(lhs, rhs, (((1,), (0,)), ((), ())), preferred_element_type=F32)
 
@@ -24,7 +28,7 @@
     nd, nf, width, factor,
     g_hbm, s_hbm, v_hbm, sw_hbm, tw_hbm,
     gv_hbm, ows, owt,
-    gext, sv, vv, sw, tw, swt, twt, st, vt, hid, part, gv, s1, r1, s2, r2, s3, r3, own3,
+    gext, sv, vv, sw, tw, st, vt, hid, part, gv, s1, r1, s2, r2, s3, r3, own3,
     in_sem, out_sem, halo_send, halo_recv, send1, recv1, send2, recv2, send3, recv3,
 ):
     nz = nf // CORES
@@ -87,7 +91,8 @@
 
     def hidden(s):
         later = jnp.concatenate([gext[s + k] for k in range(lags)], axis=1)
-        value = nn(later, twt[...])
+        weight = jnp.concatenate([tw[k * ch:(k + 1) * ch] for k in range(lags)], axis=1)
+        value = nt(later, weight)
         for b in (-1, 0, 1):
             moved = value
             if b == 1:
@@ -103,7 +108,8 @@
         moved = jnp.concatenate(
             [hid[b + 1, s, moved_rows(a)] for a in (-1, 0, 1) for b in (-1, 0, 1)], axis=1
         )
-        gv[s] = nn(moved, swt[...]).astype(BF16)
+        weight = jnp.concatenate([sw[t * ch:(t + 1) * ch] for t in range(taps)], axis=1)
+        gv[s] = nt(moved, weight).astype(BF16)
         copy = pltpu.make_async_copy(gv.at[s], gv_hbm.at[s], out_sem.at[s])
         copy.start()
         return copy
@@ -123,8 +129,6 @@
         return pl.ds(sw_rows + k * ch, ch)
 
     loads[1].wait()
-    for k in range(lags):
-        twt[k * ch:(k + 1) * ch] = tw[k * ch:(k + 1) * ch].T
     loads[0].wait()
     for s in range(early):
         hidden(s)
@@ -138,9 +142,6 @@
         vt[:, s * pixels:(s + 1) * pixels] = vv[s].T
     for t in range(taps):
         part[t * ch:(t + 1) * ch] = spatial_grad(t % 3, 2 * width - (t // 3) * width, 0, early)
-    loads[4].wait()
-    for t in range(taps):
-        swt[t * ch:(t + 1) * ch] = sw[t * ch:(t + 1) * ch].T
 
     for i in range(rim):
         @pl.when(fi < nf - 1)
@@ -229,6 +230,7 @@
             copies1.append(to_mate(len(copies1)))
             if len(copies1) > 1:
                 to_clips(len(copies1) - 2)
+    loads[4].wait()
     stores.append(grad_video(0))
     to_clips(nz - 1)
     for j in range(nz):
@@ -258,14 +260,18 @@
             halo.wait_send()
 
 
-def place(gv, gs, gt, gv_out, gs_out, gt_out, sem):
-    copies = [
-        pltpu.make_async_copy(src, dst, sem.at[i])
-        for i, (src, dst) in enumerate(((gv, gv_out), (gs, gs_out), (gt, gt_out)))
-    ]
-    for copy in copies:
+def place(gv, gs, gt, gv_out, gs_out, gt_out, gv_held, gs_held, gt_held, in_sem, out_sem):
+    frames = gv.shape[0]
+    hops = [(gv.at[s], gv_held.at[s], gv_out.at[s]) for s in range(frames)]
+    hops += [(gs, gs_held, gs_out), (gt, gt_held, gt_out)]
+    inward = [pltpu.make_async_copy(a, b, in_sem.at[i]) for i, (a, b, _) in enumerate(hops)]
+    outward = [pltpu.make_async_copy(b, c, out_sem.at[i]) for i, (_, b, c) in enumerate(hops)]
+    for copy in inward:
         copy.start()
-    for copy in copies:
+    for first, second in zip(inward, outward):
+        first.wait()
+        second.start()
+    for copy in outward:
         copy.wait()
 
 
@@ -297,8 +303,6 @@
             pltpu.VMEM((frames + lags - 1, pixels, ch), BF16),
             pltpu.VMEM(slab, BF16),
             pltpu.VMEM(slab, BF16),
-            pltpu.VMEM(spatial_w.shape, BF16),
-            pltpu.VMEM(temporal_w.shape, BF16),
             pltpu.VMEM(spatial_w.shape, BF16),
             pltpu.VMEM(temporal_w.shape, BF16),
             pltpu.VMEM((ch, frames * pixels), BF16),
@@ -339,7 +343,8 @@
         out_shape=tuple(jax.ShapeDtypeStruct(x.shape, x.dtype) for x in (gv, gs, gt)),
         in_specs=[anywhere] * 3,
         out_specs=(anywhere,) * 3,
-        scratch_shapes=[dma((3,))],
+        scratch_shapes=[pltpu.VMEM(x.shape, x.dtype) for x in (gv, gs, gt)]
+        + [dma((frames + 2,)), dma((frames + 2,))],
         compiler_params=pltpu.CompilerParams(vmem_limit_bytes=VMEM_BYTES),
         name="place_results",
     )(gv, gs, gt)

time: 65.9 us -> 31.1 us (0.47)
  Pallas kernels: 65.1 us -> 30.3 us
    pallas_call x1, Pallas kernels: 36.9 us -> 2.05 us  [local(): pl.pallas_call(place, out_shape=tuple((jax.ShapeDtypeStruct(x.shape, x.dt...]
where the time goes in v6:
time: 31.1 us; the launch traced here: 31 us
  Pallas kernels  30.3 us (97%)
  between operations  0.64 us (2%)
    pallas_call x1, Pallas kernels, local(): pl.pallas_call(functools.partial(kernel, nd, nf, width, factor), out_shap...  28.3 us
    pallas_call x1, Pallas kernels, local(): pl.pallas_call(place, out_shape=tuple((jax.ShapeDtypeStruct(x.shape, x.dt...  2.05 us

profile of v6, /device:TPU:0, one launch (start us, length us, event | category | flops | bytes accessed | tf_op | source)
XLA Modules:
  0.0 31.0 jit_solution(2647841262630035131)
XLA Ops:
  0.6 28.3 %conv_backward.1 = (bf16[4,512,256]{2,1,0:T(8,128)(2,1)}, f32[64,288]{1,0:T(8,128)}, f32[64,96]{1,0:T(8,128)}) custom-call(bf16[4,512,256]{2,1,0:T(8,128)(2,1)} %bitcast.6, bf16[4,512,256]{2,1,0:T(8,128)(2,1)} %bitcast.7, bf16[4,512,256]{2,1,0:T(8,128)(2,1)} %bitcast.8, bf16[2304,256]{1,0:T(8,128)(2,1)} %sw_hbm.1, bf16[768,256]{1,0:T(8,128)(2,1)} %tw_hbm.1), custom_call_target="tpu_custom_call" | custom-call | flops 6442450944 | bytes 4194304 | tf_op jit(solution)/shard_map/conv_backward/pallas_call | solution.py:293
  28.9 2.0 %place_results.1 = (bf16[4,512,256]{2,1,0:T(8,128)(2,1)}, f32[64,288]{1,0:T(8,128)}, f32[64,96]{1,0:T(8,128)}) custom-call(bf16[4,512,256]{2,1,0:T(8,128)(2,1)} %get-tuple-element.9.gv, f32[64,288]{1,0:T(8,128)} %get-tuple-element.10.gs, f32[64,96]{1,0:T(8,128)} %get-tuple-element.11.gt), custom_call_target="tpu_custom_call" | custom-call | tf_op jit(solution)/shard_map/place_results/pallas_call | solution.py:341

commit v7 on v6

--- a/solution.py
+++ b/solution.py
@@ -234,9 +234,11 @@
     stores.append(grad_video(0))
     to_clips(nz - 1)
     for j in range(nz):
-        if j + 1 < frames:
+        if j + 1 < frames and j != nz - 2:
             stores.append(grad_video(j + 1))
         to_owner(j)
+        if j + 1 < frames and j == nz - 2:
+            stores.append(grad_video(j + 1))
     for s in range(nz + 1, frames):
         stores.append(grad_video(s))
 

time: 31.1 us -> 31.1 us (level)
  no operation moved by 1% of the time
where the time goes in v7:
time: 31.1 us; the launch traced here: 31 us
  Pallas kernels  30.3 us (97%)
  between operations  0.64 us (2%)
    pallas_call x1, Pallas kernels, local(): pl.pallas_call(functools.partial(kernel, nd, nf, width, factor), out_shap...  28.3 us
    pallas_call x1, Pallas kernels, local(): pl.pallas_call(place, out_shape=tuple((jax.ShapeDtypeStruct(x.shape, x.dt...  2.05 us

profile of v7, /device:TPU:0, one launch (start us, length us, event | category | flops | bytes accessed | tf_op | source)
XLA Modules:
  0.0 31.0 jit_solution(9736067090367450126)
XLA Ops:
  0.6 28.3 %conv_backward.1 = (bf16[4,512,256]{2,1,0:T(8,128)(2,1)}, f32[64,288]{1,0:T(8,128)}, f32[64,96]{1,0:T(8,128)}) custom-call(bf16[4,512,256]{2,1,0:T(8,128)(2,1)} %bitcast.6, bf16[4,512,256]{2,1,0:T(8,128)(2,1)} %bitcast.7, bf16[4,512,256]{2,1,0:T(8,128)(2,1)} %bitcast.8, bf16[2304,256]{1,0:T(8,128)(2,1)} %sw_hbm.1, bf16[768,256]{1,0:T(8,128)(2,1)} %tw_hbm.1), custom_call_target="tpu_custom_call" | custom-call | flops 6442450944 | bytes 4194304 | tf_op jit(solution)/shard_map/conv_backward/pallas_call | solution.py:295
  28.9 2.0 %place_results.1 = (bf16[4,512,256]{2,1,0:T(8,128)(2,1)}, f32[64,288]{1,0:T(8,128)}, f32[64,96]{1,0:T(8,128)}) custom-call(bf16[4,512,256]{2,1,0:T(8,128)(2,1)} %get-tuple-element.9.gv, f32[64,288]{1,0:T(8,128)} %get-tuple-element.10.gs, f32[64,96]{1,0:T(8,128)} %get-tuple-element.11.gt), custom_call_target="tpu_custom_call" | custom-call | tf_op jit(solution)/shard_map/place_results/pallas_call | solution.py:343
